TPU v7x, 32 devices: a whole 2x2x4 slice. The times are simulated.
32 devices in a mesh: row: 4 (over y, x), col: 4 (over z), depth: 2 (over core).
Axes of the slice: x: 2, y: 2, z: 4, core: 2. Of those that a mesh axis runs over, the one named last changes fastest.
Arguments:
- left_store: float32 [4, 2, 16, 2, 64, 1024], P('row', 'depth', 'col'), may hold values from -6 to 6
- left_home: int32 [4, 2, 16], P('row', 'depth'), may hold values from 0 to 15, each once within a row
- up_store: float32 [4, 2, 16, 2, 64, 1024], P('col', 'depth', 'row'), may hold values from -0.3125 to 0.3125
- up_home: int32 [4, 2, 16], P('col', 'depth'), may hold values from 0 to 15, each once within a row
- targets: int32 [4, 4, 2], P('row', 'col'), may hold values from 0 to 63, as said below
- sketch: float32 [4, 4, 2, 64, 1024], P('row', 'col'), may hold values from -0.1875 to 0.1875
Outputs:
- basis: float32 [4, 4, 2, 64, 1024], P('row', 'col', 'depth')
- weights: float32 [4, 4, 2, 64, 1024], P('row', 'col', 'depth')
Inputs may be any that keep to these rules, and one draw needn't show every extreme that they name: `left_home`: for each row and depth index the entries are the store positions 0 to 15, each once. `up_home`: for each col and depth index the entries are the store positions 0 to 15, each once. `targets`: the 2 entries of one row and col index are distinct.
All inputs are finite; a program needn't handle non-finite values.
Results may differ from a plain program's by a relative error of at most 0.0003.
Values sent between devices are 32-bit elements; how exact they have to be, the bound alone decides.
A program may use at most 128 MiB of HBM per device.

v0:
```python
import math

import jax
import jax.numpy as jnp
from jax import lax
from jax.sharding import PartitionSpec as P

KD = 2
RB = 8
CB = 8


def orthonormal(sample):
    gram_mat = jnp.einsum("pat,pbt->pab", sample, sample, precision=lax.Precision.HIGHEST)
    factor_low = jnp.linalg.cholesky(gram_mat)
    return lax.linalg.triangular_solve(factor_low, sample, left_side=True, lower=True)


def shards(left_store, left_home, up_store, up_home, targets, sketch):
    high = lax.Precision.HIGHEST
    left_local = left_store[0, 0]
    up_local = up_store[0, 0]
    left_table = left_home[0, 0]
    up_table = up_home[0, 0]
    left_all = lax.all_gather(left_local, "col", axis=0, tiled=True)
    up_all = lax.all_gather(up_local, "row", axis=0, tiled=True)
    left_pairs = jnp.take(left_all, left_table, axis=0)
    up_pairs = jnp.take(up_all, up_table, axis=0)
    chosen = targets[0, 0]
    block_row = chosen // CB
    block_col = chosen % CB
    row_pairs = jnp.take(left_pairs.reshape((RB, KD) + left_local.shape[1:]), block_row, axis=0)
    col_pairs = jnp.take(up_pairs.reshape((CB, KD) + up_local.shape[1:]), block_col, axis=0)
    row_basis = row_pairs[:, :, 0]
    row_coef = row_pairs[:, :, 1]
    col_coef = col_pairs[:, :, 0]
    col_basis = col_pairs[:, :, 1]
    test_rows = sketch[0, 0]
    middle = jnp.einsum("pkat,pkbt->pkab", row_coef, col_coef, precision=high)
    test_side = jnp.einsum("pat,pkbt->pkab", test_rows, col_basis, precision=high)
    folded = jnp.einsum("pkab,pkcb->pkac", test_side, middle, precision=high)
    sample_part = jnp.einsum("pkac,pkct->pat", folded, row_basis, precision=high)
    own_sketch = lax.psum_scatter(sample_part, "depth", scatter_dimension=0, tiled=True)
    own_basis = orthonormal(own_sketch)
    bases = lax.all_gather(own_basis, "depth", axis=0, tiled=True)
    inner_prod = jnp.einsum("pat,pkct->pkac", bases, row_basis, precision=high)
    turned = jnp.einsum("pkac,pkcb->pkab", inner_prod, middle, precision=high)
    project_part = jnp.einsum("pkab,pkbt->pat", turned, col_basis, precision=high)
    projected = lax.psum_scatter(project_part, "depth", scatter_dimension=0, tiled=True)
    root_tile = math.sqrt(test_rows.shape[-1])
    return ((own_basis * root_tile)[None, None], (projected / root_tile)[None, None])


def solution(mesh):
    return jax.shard_map(
        shards,
        mesh=mesh,
        in_specs=(
            P("row", "depth", "col", None, None, None),
            P("row", "depth", None),
            P("col", "depth", "row", None, None, None),
            P("col", "depth", None),
            P("row", "col", None),
            P("row", "col", None, None, None),
        ),
        out_specs=(P("row", "col", "depth", None, None), P("row", "col", "depth", None, None)),
        check_vma=False,
    )
```

profile of v0, /device:TPU:0, one launch (start us, length us, event | category | flops | bytes accessed | tf_op | source)
XLA Modules:
  0.0 326.1 jit_solution(14357726791905999207)
XLA Ops:
  7.2 0.0 copy-start
  7.2 0.0 all-gather.8.cloned.1.call-start
  7.2 0.0 copy-start.3
  7.2 0.0 copy-start.2
  7.2 0.0 copy-start.4
  7.3 0.7 all-gather.8.cloned.1.call-update
  7.9 0.0 all-gather.6.cloned.1.call-start
  8.0 0.7 all-gather.6.cloned.1.call-update
  8.7 0.0 reduce-scatter.3.cloned.1.call-start
  8.7 0.0 copy-done.3
  8.7 0.0 copy-done.2
  8.8 0.0 copy-done.4
  8.9 153.1 %all-gather.8.cloned.1.call-done = f32[1,1,16,2,64,1024]{5,4,3,1,0,2:T(8,128)} async-done(((f32[1,1,4,2,64,1024]{5,4,3,1,0,2:T(8,128)}), f32[1,1,16,2,64,1024]{5,4,3,1,0,2:T(8,128)}) %all-gather.8.cloned.1.call-update) | async-done | bytes 8388624 | tf_op jit(solution)/shard_map/all_gather | solution.py:25
  162.0 8.3 %gather_fusion.2 = f32[16,2,64,1024]{3,2,1,0:T(8,128)} fusion(f32[16,2,64,1024]{3,2,1,0:T(8,128)} %bitcast.95, s32[1024]{0:T(1024)S(1)} %pad_clamp_fusion.1), kind=kCustom, calls=%fused_computation.2.clone | custom fusion | bytes 16777280 | tf_op jit(solution)/shard_map/jit(_take)/gather | solution.py:27
  170.3 9.7 %broadcast_select_fusion = f32[16,2,64,1024]{3,2,1,0:T(8,128)} fusion(f32[16,2,64,1024]{3,2,1,0:T(8,128)} %gather_fusion.2, pred[16]{0:T(512)(128)(4,1)S(1)} %compare_and_fusion.1), kind=kLoop, calls=%fused_computation.4 | loop fusion | flops 2097152 | bytes 16777232 | tf_op jit(solution)/shard_map/jit(_take)/select_n | solution.py:27
  180.0 5.4 %gather_fusion.3 = f32[2,2,2,64,1024]{4,3,2,1,0:T(8,128)} fusion(f32[8,2,2,64,1024]{4,3,2,1,0:T(8,128)} %bitcast.92, s32[1024]{0:T(1024)S(1)} %pad_clamp_fusion), kind=kCustom, calls=%fused_computation.3.clone | custom fusion | bytes 4194312 | tf_op jit(solution)/shard_map/jit(_take)/gather | solution.py:32
  185.4 64.3 %all-gather.6.cloned.1.call-done = f32[1,1,16,2,64,1024]{5,4,3,1,0,2:T(8,128)} async-done(((f32[1,1,4,2,64,1024]{5,4,3,1,0,2:T(8,128)}), f32[1,1,16,2,64,1024]{5,4,3,1,0,2:T(8,128)}) %all-gather.6.cloned.1.call-update) | async-done | bytes 8388624 | tf_op jit(solution)/shard_map/all_gather | solution.py:26
  249.7 7.7 %gather_fusion = f32[16,2,64,1024]{3,2,1,0:T(8,128)} fusion(f32[16,2,64,1024]{3,2,1,0:T(8,128)} %bitcast.94, s32[1024]{0:T(1024)S(1)} %pad_clamp_fusion.3), kind=kCustom, calls=%fused_computation.clone | custom fusion | bytes 16777280 | tf_op jit(solution)/shard_map/jit(_take)/gather | solution.py:28
  257.4 8.6 %broadcast_select_fusion.1 = f32[16,2,64,1024]{3,2,1,0:T(8,128)} fusion(f32[16,2,64,1024]{3,2,1,0:T(8,128)} %gather_fusion, pred[16]{0:T(512)(128)(4,1)S(1)} %compare_and_fusion.3), kind=kLoop, calls=%fused_computation.5 | loop fusion | flops 2097152 | bytes 16777232 | tf_op jit(solution)/shard_map/jit(_take)/select_n | solution.py:28
  266.0 5.4 %gather_fusion.1 = f32[2,2,2,64,1024]{4,3,2,1,0:T(8,128)} fusion(f32[8,2,2,64,1024]{4,3,2,1,0:T(8,128)} %bitcast.93, s32[1024]{0:T(1024)S(1)} %pad_clamp_fusion.2), kind=kCustom, calls=%fused_computation.1.clone | custom fusion | bytes 4194312 | tf_op jit(solution)/shard_map/jit(_take)/gather | solution.py:33
  271.4 2.8 copy_select_fusion
  274.2 0.0 copy-start.1
  274.2 0.0 copy-done
  274.2 1.6 fusion.1
  275.8 1.1 fusion
  276.9 0.3 fusion.11
  277.2 0.0 copy-done.1
  277.2 1.5 convolution_bitcast_fusion.1
  278.7 0.0 reduce-scatter.3.cloned.1.call-update
  278.8 0.0 reduce-scatter.5.cloned.1.call-start
  278.8 8.1 %reduce-scatter.3.cloned.1.call-done = f32[1,64,1024]{2,1,0:T(8,128)} async-done(((f32[2,64,1024]{2,1,0:T(8,128)}), f32[1,64,1024]{2,1,0:T(8,128)}) %reduce-scatter.3.cloned.1.call-update) | async-done | bytes 262160 | tf_op jit(solution)/shard_map/reduce_scatter | solution.py:43
  286.9 1.4 fusion.6
  288.3 0.1 copy.20
  288.3 5.8 %custom-call.7 = f32[1,64,64]{2,1,0:T(8,128)S(1)} custom-call(f32[1,64,64]{2,1,0:T(8,128)S(1)} %fusion.9), custom_call_target="Cholesky" | custom-call | tf_op jit(solution)/shard_map/jit(cholesky)/cholesky | solution.py:15
  294.2 0.6 compare_reduce_fusion
  294.9 0.7 fusion.8
  295.5 4.9 %custom-call.8 = f32[1,1,64,64]{2,3,1,0:T(8,128)S(1)} custom-call(f32[1,1,64,64]{3,2,1,0:T(8,128)S(1)} %fusion.8), custom_call_target="InvertDiagBlocksLowerTriangular" | custom-call | tf_op jit(solution)/shard_map/triangular_solve | solution.py:16
  300.4 1.4 fusion.4
  301.8 2.2 all-gather.2
  304.0 2.8 fusion.2
  306.8 0.3 fusion.12
  307.1 1.5 convolution_bitcast_fusion
  308.6 0.0 reduce-scatter.5.cloned.1.call-update
  308.6 0.7 multiply_bitcast_fusion.1
  309.3 8.5 %reduce-scatter.5.cloned.1.call-done = f32[1,64,1024]{2,1,0:T(8,128)} async-done(((f32[2,64,1024]{2,1,0:T(8,128)}), f32[1,64,1024]{2,1,0:T(8,128)}) %reduce-scatter.5.cloned.1.call-update) | async-done | bytes 262160 | tf_op jit(solution)/shard_map/reduce_scatter | solution.py:49
  317.9 1.7 multiply_bitcast_fusion
  (11 shorter events, 0.1 us)
Async XLA Ops:
  7.2 267.0 %copy-start = (f32[1,1,2,64,1024]{4,3,2,1,0:T(8,128)S(1)}, f32[1,1,2,64,1024]{4,3,2,1,0:T(8,128)}, u32[]{:S(2)}) copy-start(f32[1,1,2,64,1024]{4,3,2,1,0:T(8,128)} %param.15) | copy-start | bytes 1572868
  7.2 154.8 %all-gather.8.cloned.1.call-start = ((), (), s32[]{:S(2)}) async-start(), calls=%async_computation.5 | async-start | bytes 10485760 | tf_op jit(solution)/shard_map/all_gather | solution.py:25
  7.2 1.5 copy-start.3
  7.2 1.5 copy-start.2
  7.2 1.5 copy-start.4
  7.9 241.8 %all-gather.6.cloned.1.call-start = ((), (), s32[]{:S(2)}) async-start(), calls=%async_computation.4 | async-start | bytes 10485760 | tf_op jit(solution)/shard_map/all_gather | solution.py:26
  8.7 278.2 %reduce-scatter.3.cloned.1.call-start = ((), (), s32[]{:S(2)}) async-start(), calls=%async_computation.2 | async-start | bytes 786432 | tf_op jit(solution)/shard_map/reduce_scatter | solution.py:43
  274.2 3.1 copy-start.1
  278.8 39.1 %reduce-scatter.5.cloned.1.call-start = ((), (), s32[]{:S(2)}) async-start(), calls=%async_computation.3 | async-start | bytes 786432 | tf_op jit(solution)/shard_map/reduce_scatter | solution.py:49
Sparse Core Ops, SparseCore 0:
  9.6 152.3 all-gather.7
  163.8 85.8 all-gather.5
  278.9 7.9 reduce-scatter.2
  308.7 9.1 reduce-scatter.4
where the time goes:
time: 327 us; the launch traced here: 326 us
  waiting for transfers between devices  235 us (72%)
  other arithmetic  35.6 us (11%)
  local copies, waits for them, and re-layouts  26.9 us (8%)
  between operations  14 us (4%)
  matrix products  11.9 us (4%)
    all_gather x1, waiting for transfers between devices, shards(): left_all = lax.all_gather(left_local, 'col', axis=0, tiled=True)  153 us
    all_gather x1, waiting for transfers between devices, shards(): up_all = lax.all_gather(up_local, 'row', axis=0, tiled=True)  64.3 us
    select_n x2, other arithmetic, shards(): left_pairs = jnp.take(left_all, left_table, axis=0)  9.72 us
    select_n x2, other arithmetic, shards(): up_pairs = jnp.take(up_all, up_table, axis=0)  8.62 us
    reduce_scatter x1, waiting for transfers between devices, shards(): lax.psum_scatter(project_part, 'depth', scatter_dimension=0, tiled=True)  8.55 us
    gather x1, local copies, waits for them, and re-layouts, shards(): left_pairs = jnp.take(left_all, left_table, axis=0)  8.3 us
    reduce_scatter x1, waiting for transfers between devices, shards(): lax.psum_scatter(sample_part, 'depth', scatter_dimension=0, tiled=True)  8.05 us
    gather x1, local copies, waits for them, and re-layouts, shards(): up_pairs = jnp.take(up_all, up_table, axis=0)  7.69 us
  transfers between devices with their start and end apart: 4, of which 4 were waited for; matrix products, arithmetic and copies ran while one was open for 7% of the time, Pallas kernels for 0%

commit v1 on v0

v1 whole, which is shorter than its diff:
```python
import functools
import math

import jax
import jax.numpy as jnp
from jax import lax
from jax.experimental import pallas as pl
from jax.experimental.pallas import tpu as pltpu
from jax.sharding import PartitionSpec as P

KD = 2
RB = 8
CB = 8
PIECES = 4
AHEAD = 2
HIGH = lax.Precision.HIGHEST


def mul(a, b):
    return lax.dot_general(a, b, (((1,), (0,)), ((), ())), precision=HIGH, preferred_element_type=jnp.float32)


def mul_t(a, b):
    return lax.dot_general(a, b, (((1,), (1,)), ((), ())), precision=HIGH, preferred_element_type=jnp.float32)


def inverse_factor(grams):
    n = grams[0].shape[0]
    row = lax.broadcasted_iota(jnp.int32, (n, n), 0)
    col = lax.broadcasted_iota(jnp.int32, (n, n), 1)
    eye = (row == col).astype(jnp.float32)
    work = [[jnp.concatenate([g, eye], axis=1)[i : i + 8] for i in range(0, n, 8)] for g in grams]
    sub = lax.broadcasted_iota(jnp.int32, (8, 1), 0)
    for j in range(n - 1):
        top, inside = j // 8, j % 8
        for blocks in work:
            line = blocks[top][inside : inside + 1, :]
            line = line / line[:, j : j + 1]
            for b in range(top, n // 8):
                factor = blocks[b][:, j : j + 1]
                if b == top:
                    if inside == 7:
                        continue
                    factor = jnp.where(sub > inside, factor, 0.0)
                blocks[b] = blocks[b] - factor * line
    results = []
    for blocks in work:
        whole = jnp.concatenate(blocks, axis=0)
        pivots = jnp.sum(whole[:, :n] * eye, axis=1, keepdims=True)
        results.append(whole[:, n:] / jnp.sqrt(pivots))
    return results


def ring_maps(n):
    side = math.isqrt(n)
    if side * side != n:
        return (lambda r: r), (lambda q: q)

    def swap(r):
        y, x = r // side, r % side
        return y * side + jnp.where(y % 2 == 0, x, side - 1 - x)

    return swap, swap


def kernel(sizes, tgt, lhome, uhome, left, up, sketch, out_b, out_w, *scratch):
    n_row, n_col, n_depth = sizes
    pieces = PIECES
    lbuf, scratch = scratch[:pieces], scratch[pieces:]
    ubuf, scratch = scratch[:pieces], scratch[pieces:]
    pack, scratch = scratch[:pieces], scratch[pieces:]
    (acc_m, acc_v, zpart, zrecv, hpart, hrecv, inner, linv,
     loc_sem, zs_sem, zr_sem, rs_sem, rr_sem, ks_sem, kr_sem, xs_sem, xr_sem) = scratch
    lheld, uheld = left.shape[0], up.shape[0]
    tiles, rank, width = sketch.shape
    piece = width // pieces
    slots = tiles * KD
    row, col, dep = lax.axis_index("row"), lax.axis_index("col"), lax.axis_index("depth")
    other = n_depth - 1 - dep
    to_ring, from_ring = ring_maps(n_row)
    spot = to_ring(row)
    half_way = n_row // 2

    def ring_row(offset):
        return from_ring((spot + offset + n_row) % n_row)

    right, left_of = (row, col + 1, dep), (row, col - 1, dep)
    after, before = (ring_row(1), col, dep), (ring_row(-1), col, dep)
    twin = (row, col, other)
    mesh_id = pl.DeviceIdType.MESH

    def local(t):
        cut = pl.ds(t * piece, piece)
        return (
            pltpu.make_async_copy(left.at[:, :, :, cut], lbuf[t].at[pl.ds(col * lheld, lheld)], loc_sem.at[0, t]),
            pltpu.make_async_copy(up.at[:, :, :, cut], ubuf[t].at[pl.ds(row * uheld, uheld)], loc_sem.at[1, t]),
        )

    def line_copy(way, dist, t):
        source = col - (dist - 1) if way == 0 else col + (dist - 1)
        view = lbuf[t].at[pl.ds(source * lheld, lheld)]
        return pltpu.make_async_remote_copy(
            src_ref=view, dst_ref=view, send_sem=zs_sem.at[way, dist - 1, t], recv_sem=zr_sem.at[way, dist - 1, t],
            device_id=right if way == 0 else left_of, device_id_type=mesh_id)

    def slot_copy(way, t):
        return pltpu.make_async_remote_copy(
            src_ref=pack[t].at[way], dst_ref=lbuf[t].at[pl.ds(n_col * lheld, slots)], send_sem=ks_sem.at[way, t],
            recv_sem=kr_sem.at[way, t], device_id=right if way == 0 else left_of, device_id_type=mesh_id)

    def ring_copy(way, dist, t):
        source = ring_row(1 - dist if way == 0 else dist - 1)
        view = ubuf[t].at[pl.ds(source * uheld, uheld)]
        if n_row % 2 == 0 and dist == half_way:
            view = ubuf[t].at[pl.ds(source * uheld, uheld), way]
        return pltpu.make_async_remote_copy(
            src_ref=view, dst_ref=view, send_sem=rs_sem.at[way, dist - 1, t], recv_sem=rr_sem.at[way, dist - 1, t],
            device_id=after if way == 0 else before, device_id_type=mesh_id)

    def can_send(way, dist):
        if way == 0:
            end = col < n_col - 1 if dist == 1 else col < n_col - 2
            return jnp.logical_and(col - (dist - 1) >= 0, end)
        end = col > 0 if dist == 1 else col > 1
        return jnp.logical_and(col + (dist - 1) <= n_col - 1, end)

    def receives(way, dist):
        if way == 0:
            if dist == 1:
                return col >= 1
            return jnp.logical_and(col - dist >= 0, col < n_col - 1)
        if dist == 1:
            return col <= n_col - 2
        return jnp.logical_and(col + dist <= n_col - 1, col > 0)

    far = max(n_col - 2, 1) if n_col > 1 else 0

    def left_index(c, p, k, packed):
        pos = lhome[(tgt[c, p] // CB) * KD + k]
        if not packed or n_col < 3:
            return pos
        source = pos // lheld
        by_slot = jnp.logical_or(
            jnp.logical_and(col == 0, source >= 2), jnp.logical_and(col == n_col - 1, source <= n_col - 3))
        return jnp.where(by_slot, n_col * lheld + p * KD + k, pos)

    def up_index(p, k):
        return uhome[(tgt[col, p] % CB) * KD + k]

    def send_own(t):
        for copy in local(t):
            copy.wait()
        for way in range(2):
            if n_col > 1:
                @pl.when(can_send(way, 1))
                def _():
                    line_copy(way, 1, t).start()
            if n_row > 1:
                ring_copy(way, 1, t).start()

    def fill_slots(t):
        for way in range(2):
            turn = col == n_col - 2 if way == 0 else col == 1
            goal = n_col - 1 if way == 0 else 0

            @pl.when(turn)
            def _():
                for p in range(tiles):
                    for k in range(KD):
                        pack[t][way, p * KD + k] = lbuf[t][left_index(goal, p, k, False)]
                slot_copy(way, t).start()

    def await_slots(t):
        for way in range(2):
            @pl.when(col == n_col - 1 if way == 0 else col == 0)
            def _():
                slot_copy(way, t).wait_recv()

    def accumulate(t):
        for p in range(tiles):
            tests = sketch[p, :, t * piece : (t + 1) * piece]
            for k in range(KD):
                coef = lbuf[t][left_index(col, p, k, True), 1]
                pair = ubuf[t].at[up_index(p, k)]
                middle = mul_t(coef, pair[0])
                tested = mul_t(tests, pair[1])
                if t == 0:
                    acc_m[p, k] = middle
                    acc_v[p, k] = tested
                else:
                    acc_m[p, k] += middle
                    acc_v[p, k] += tested

    for t in range(pieces):
        for copy in local(t):
            copy.start()

    barrier = pltpu.get_barrier_semaphore()
    peers = [twin] + ([after, before] if n_row > 1 else [])
    for peer in peers:
        pl.semaphore_signal(barrier, inc=1, device_id=peer, device_id_type=mesh_id)
    greeted = len(peers)
    if n_col > 1:
        for able, peer in ((col < n_col - 1, right), (col > 0, left_of)):
            @pl.when(able)
            def _():
                pl.semaphore_signal(barrier, inc=1, device_id=peer, device_id_type=mesh_id)
            greeted = greeted + able.astype(jnp.int32)
    pl.semaphore_wait(barrier, greeted)

    for t in range(min(AHEAD, pieces)):
        send_own(t)
    lag = max(n_col - 2, half_way - 1, 0)
    for step in range(pieces + lag):
        for dist in range(1, max(far, half_way) + 1):
            t = step - (dist - 1)
            if not 0 <= t < pieces:
                continue
            for way in range(2):
                if dist <= far:
                    @pl.when(receives(way, dist))
                    def _():
                        line_copy(way, dist, t).wait_recv()
                    if dist + 1 <= far:
                        @pl.when(can_send(way, dist + 1))
                        def _():
                            line_copy(way, dist + 1, t).start()
                if n_row > 1 and dist <= half_way:
                    ring_copy(way, dist, t).wait_recv()
                    if dist + 1 <= half_way:
                        ring_copy(way, dist + 1, t).start()
        if AHEAD + step < pieces:
            send_own(AHEAD + step)
        if n_col > 2:
            if 0 <= step - (n_col - 3) < pieces:
                fill_slots(step - (n_col - 3))
            if 0 <= step - (n_col - 2) < pieces:
                await_slots(step - (n_col - 2))
        if 0 <= step - lag < pieces:
            accumulate(step - lag)

    def row_basis(t, p):
        return jnp.concatenate([lbuf[t][left_index(col, p, k, True), 0] for k in range(KD)], axis=0)

    def twin_copy(which, src, dst):
        return pltpu.make_async_remote_copy(
            src_ref=src, dst_ref=dst, send_sem=xs_sem.at[which], recv_sem=xr_sem.at[which], device_id=twin, device_id_type=mesh_id)

    z_copies = [twin_copy(p, zpart.at[p], zrecv.at[p]) for p in range(tiles)]
    for p in range(tiles):
        folded = jnp.concatenate([mul_t(acc_v[p, k], acc_m[p, k]) for k in range(KD)], axis=1)
        for t in range(pieces):
            zpart[p, :, t * piece : (t + 1) * piece] = mul(folded, row_basis(t, p))
        z_copies[p].start()
    grams, sides = [], []
    for p in range(tiles):
        z_copies[p].wait()
        zpart[p] = zpart[p] + zrecv[p]
        gram, side = None, None
        for t in range(pieces):
            z = zpart[p, :, t * piece : (t + 1) * piece]
            g, s = mul_t(z, z), mul_t(z, row_basis(t, p))
            gram, side = (g, s) if t == 0 else (gram + g, side + s)
        grams.append(gram)
        sides.append(side)
    inverses = inverse_factor(grams)
    for p in range(tiles):
        linv[p] = inverses[p]
        turned = mul(inverses[p], sides[p])
        inner[p] = jnp.concatenate(
            [mul(turned[:, k * rank : (k + 1) * rank], acc_m[p, k]) for k in range(KD)], axis=1)

    owned = tiles // n_depth
    root = math.sqrt(width)

    def project(p, t):
        cols = jnp.concatenate([ubuf[t][up_index(p, k), 1] for k in range(KD)], axis=0)
        return mul(inner[p], cols)

    h_copy = twin_copy(tiles, hpart, hrecv)
    for i in range(owned):
        for t in range(pieces):
            hpart[i, :, t * piece : (t + 1) * piece] = project(other * owned + i, t)
    h_copy.start()
    for i in range(owned):
        p = dep * owned + i
        for t in range(pieces):
            cut = slice(t * piece, (t + 1) * piece)
            out_b[i, :, cut] = mul(linv[p], zpart[p, :, cut]) * root
            out_w[i, :, cut] = project(p, t)
    h_copy.wait()
    for i in range(owned):
        out_w[i] = (out_w[i] + hrecv[i]) / root

    for t in range(pieces):
        for way in range(2):
            for dist in range(1, far + 1):
                @pl.when(can_send(way, dist))
                def _():
                    line_copy(way, dist, t).wait_send()
            if n_col > 2:
                @pl.when(col == n_col - 2 if way == 0 else col == 1)
                def _():
                    slot_copy(way, t).wait_send()
            if n_row > 1:
                for dist in range(1, half_way + 1):
                    ring_copy(way, dist, t).wait_send()


def solution(mesh):
    sizes = tuple(mesh.shape[a] for a in ("row", "col", "depth"))
    n_row, n_col, n_depth = sizes

    def shards(left_store, left_home, up_store, up_home, targets, sketch):
        lheld, _, rank, width = left_store.shape[2:]
        uheld = up_store.shape[2]
        tiles = targets.shape[2]
        slots = tiles * KD
        owned = tiles // n_depth
        piece = width // PIECES
        all_targets = lax.all_gather(targets[0], "col", axis=0, tiled=True)
        f32 = jnp.float32
        dma = pltpu.SemaphoreType.DMA
        far, half_way = max(n_col - 2, 1), max(n_row // 2, 1)
        out = jax.ShapeDtypeStruct((owned, rank, width), f32)
        vmem, smem = pl.BlockSpec(memory_space=pltpu.VMEM), pl.BlockSpec(memory_space=pltpu.SMEM)
        anywhere = pl.BlockSpec(memory_space=pl.ANY)
        basis, weights = pl.pallas_call(
            functools.partial(kernel, sizes),
            out_shape=(out, out),
            in_specs=[smem, smem, smem, anywhere, anywhere, vmem],
            out_specs=(vmem, vmem),
            scratch_shapes=[pltpu.VMEM((n_col * lheld + slots, 2, rank, piece), f32)] * PIECES
            + [pltpu.VMEM((n_row * uheld, 2, rank, piece), f32)] * PIECES
            + [pltpu.VMEM((2, slots, 2, rank, piece), f32)] * PIECES
            + [
                pltpu.VMEM((tiles, KD, rank, rank), f32),
                pltpu.VMEM((tiles, KD, rank, rank), f32),
                pltpu.VMEM((tiles, rank, width), f32),
                pltpu.VMEM((tiles, rank, width), f32),
                pltpu.VMEM((owned, rank, width), f32),
                pltpu.VMEM((owned, rank, width), f32),
                pltpu.VMEM((tiles, rank, KD * rank), f32),
                pltpu.VMEM((tiles, rank, rank), f32),
                dma((2, PIECES)),
                dma((2, far, PIECES)),
                dma((2, far, PIECES)),
                dma((2, half_way, PIECES)),
                dma((2, half_way, PIECES)),
                dma((2, PIECES)),
                dma((2, PIECES)),
                dma((tiles + 1,)),
                dma((tiles + 1,)),
            ],
            compiler_params=pltpu.CompilerParams(
                collective_id=0, has_side_effects=True, vmem_limit_bytes=48 * 1024 * 1024),
        )(all_targets, left_home[0, 0], up_home[0, 0], left_store[0, 0], up_store[0, 0], sketch[0, 0])
        return basis[None, None], weights[None, None]

    return jax.shard_map(
        shards,
        mesh=mesh,
        in_specs=(
            P("row", "depth", "col", None, None, None),
            P("row", "depth", None),
            P("col", "depth", "row", None, None, None),
            P("col", "depth", None),
            P("row", "col", None),
            P("row", "col", None, None, None),
        ),
        out_specs=(P("row", "col", "depth", None, None), P("row", "col", "depth", None, None)),
        check_vma=False,
    )
```

time: 327 us -> 137 us (0.42)
  waiting for transfers between devices: 235 us -> 0 us
  Pallas kernels: 0 us -> 116 us
  other arithmetic: 35.6 us -> 0 us
  local copies, waits for them, and re-layouts: 26.9 us -> 6.94 us
  between operations: 14 us -> 0.64 us
  matrix products: 11.9 us -> 0 us
  blocking collectives: 2.18 us -> 12.7 us
    all_gather x2 -> x0, waiting for transfers between devices: 217 us -> none  [the longest x1 153 us: shards(): left_all = lax.all_gather(left_local, 'col', axis=0, tiled=True)]
    pallas_call x0 -> x1, Pallas kernels: none -> 116 us  [shards(): pl.pallas_call(functools.partial(kernel, sizes), out_shape=(out, out), in...]
    gather x4 -> x0, local copies, waits for them, and re-layouts: 26.8 us -> none  [the longest x1 8.3 us: shards(): left_pairs = jnp.take(left_all, left_table, axis=0)]
    select_n x5 -> x0, other arithmetic: 21.1 us -> none  [the longest x2 9.72 us: shards(): left_pairs = jnp.take(left_all, left_table, axis=0)]
    reduce_scatter x2 -> x0, waiting for transfers between devices: 16.6 us -> none  [the longest x1 8.55 us: shards(): lax.psum_scatter(project_part, 'depth', scatter_dimension=0, tiled=True)]
    another operation x5 -> x0, other arithmetic: 12.1 us -> none  [the longest x3 6.52 us: orthonormal(): factor_low = jnp.linalg.cholesky(gram_mat)]
    all_gather x1, blocking collectives: 2.18 us -> 12.7 us  [shards(): all_targets = lax.all_gather(targets[0], 'col', axis=0, tiled=True)]
    dot_general x8 -> x0, matrix products: 10.5 us -> none  [the longest x1 2.84 us: shards(): inner_prod = jnp.einsum('pat,pkct->pkac', bases, row_basis, precision=high)]
  transfers between devices with their start and end apart: 4 -> 0, of which waited for: 4 -> 0; matrix products, arithmetic and copies ran while one was open for 7% -> 0% of each run, Pallas kernels for 0% -> 0%
where the time goes in v1:
time: 137 us
  Pallas kernels  116 us (85%)
  blocking collectives  12.7 us (9%)
  local copies, waits for them, and re-layouts  6.94 us (5%)
    pallas_call x1, Pallas kernels, shards(): pl.pallas_call(functools.partial(kernel, sizes), out_shape=(out, out), in...  116 us
    all_gather x1, blocking collectives, shards(): all_targets = lax.all_gather(targets[0], 'col', axis=0, tiled=True)  12.7 us
    unnamed x12, local copies, waits for them, and re-layouts  6.94 us

profile of v1, /device:TPU:0, one launch (start us, length us, event | category | flops | bytes accessed | tf_op | source)
XLA Modules:
  0.0 136.5 jit_solution(4286775896607198719)
XLA Ops:
  0.6 12.7 %all-gather = s32[4,1,2]{2,1,0:T(1,128)S(1)} all-gather(s32[1,1,2]{2,1,0:T(1,128)} %param.10), channel_id=2, replica_groups=mesh['row'=4,'col'=4,'depth'=2] {'col'}, dimensions={0}, use_global_device_ids=true | all-gather | bytes 40 | tf_op jit(solution)/shard_map/all_gather | solution.py:321
  13.3 0.0 copy-start
  13.3 1.6 %copy-done = f32[1,1,4,2,64,1024]{5,4,3,2,1,0:T(8,128)S(1)} copy-done((f32[1,1,4,2,64,1024]{5,4,3,2,1,0:T(8,128)S(1)}, f32[1,1,4,2,64,1024]{5,4,3,2,1,0:T(8,128)}, u32[]{:S(2)}) %copy-start) | copy-done | bytes 2097176
  14.9 0.0 copy-start.1
  14.9 1.6 %copy-done.1 = f32[1,1,4,2,64,1024]{5,4,3,2,1,0:T(8,128)S(1)} copy-done((f32[1,1,4,2,64,1024]{5,4,3,2,1,0:T(8,128)S(1)}, f32[1,1,4,2,64,1024]{5,4,3,2,1,0:T(8,128)}, u32[]{:S(2)}) %copy-start.1) | copy-done | bytes 2097176
  16.5 0.0 copy-start.2
  16.5 1.0 copy-done.2
  17.6 0.0 copy-start.3
  17.6 0.7 copy-done.3
  18.2 0.0 copy-start.4
  18.2 0.7 copy-done.4
  18.9 116.2 %shard_map.77 = (f32[1,64,1024]{2,1,0:T(8,128)S(1)}, f32[1,64,1024]{2,1,0:T(8,128)S(1)}) custom-call(s32[4,2]{1,0:T(4,128)S(1)} %bitcast.13, s32[16]{0:T(128)S(1)} %bitcast.14, s32[16]{0:T(128)S(1)} %bitcast.15, f32[4,2,64,1024]{3,2,1,0:T(8,128)S(1)} %bitcast.8, f32[4,2,64,1024]{3,2,1,0:T(8,128)S(1)} %bitcast.9, f32[2,64,1024]{2,1,0:T(8,128)S(1)} %bitcast.10), custom_call_target="tpu_custom_call" | custom-call | tf_op jit(solution)/shard_map/pallas_call | solution.py:328
  135.1 0.7 copy.15
  135.8 0.7 copy.16
Async XLA Ops:
  13.3 1.6 %copy-start = (f32[1,1,4,2,64,1024]{5,4,3,2,1,0:T(8,128)S(1)}, f32[1,1,4,2,64,1024]{5,4,3,2,1,0:T(8,128)}, u32[]{:S(2)}) copy-start(f32[1,1,4,2,64,1024]{5,4,3,2,1,0:T(8,128)} %param.6) | copy-start | bytes 6291460
  14.9 1.6 %copy-start.1 = (f32[1,1,4,2,64,1024]{5,4,3,2,1,0:T(8,128)S(1)}, f32[1,1,4,2,64,1024]{5,4,3,2,1,0:T(8,128)}, u32[]{:S(2)}) copy-start(f32[1,1,4,2,64,1024]{5,4,3,2,1,0:T(8,128)} %param.8) | copy-start | bytes 6291460
  16.5 1.0 copy-start.2
  17.6 0.7 copy-start.3
  18.2 0.7 copy-start.4

commit v2 on v1

--- a/solution.py
+++ b/solution.py
@@ -63,14 +63,15 @@
     return swap, swap
 
 
-def kernel(sizes, tgt, lhome, uhome, left, up, sketch, out_b, out_w, *scratch):
+def kernel(sizes, tgt_in, lhome_in, uhome_in, left_in, up_in, sketch_in, out_b, out_w, *scratch):
     n_row, n_col, n_depth = sizes
     pieces = PIECES
     lbuf, scratch = scratch[:pieces], scratch[pieces:]
     ubuf, scratch = scratch[:pieces], scratch[pieces:]
     pack, scratch = scratch[:pieces], scratch[pieces:]
     (acc_m, acc_v, zpart, zrecv, hpart, hrecv, inner, linv,
-     loc_sem, zs_sem, zr_sem, rs_sem, rr_sem, ks_sem, kr_sem, xs_sem, xr_sem) = scratch
+     tgt, tgt_end, lhome, uhome, sketch, tab_sem, ts_sem, tr_sem, loc_sem, zs_sem, zr_sem, rs_sem, rr_sem, ks_sem, kr_sem, xs_sem, xr_sem) = scratch
+    left, up = left_in.at[0, 0], up_in.at[0, 0]
     lheld, uheld = left.shape[0], up.shape[0]
     tiles, rank, width = sketch.shape
     piece = width // pieces
@@ -135,8 +136,8 @@
 
     far = max(n_col - 2, 1) if n_col > 1 else 0
 
-    def left_index(c, p, k, packed):
-        pos = lhome[(tgt[c, p] // CB) * KD + k]
+    def left_index(table, p, k, packed):
+        pos = lhome[0, 0, (table[0, 0, p] // CB) * KD + k]
         if not packed or n_col < 3:
             return pos
         source = pos // lheld
@@ -145,7 +146,7 @@
         return jnp.where(by_slot, n_col * lheld + p * KD + k, pos)
 
     def up_index(p, k):
-        return uhome[(tgt[col, p] % CB) * KD + k]
+        return uhome[0, 0, (tgt[0, 0, p] % CB) * KD + k]
 
     def send_own(t):
         for copy in local(t):
@@ -161,13 +162,14 @@
     def fill_slots(t):
         for way in range(2):
             turn = col == n_col - 2 if way == 0 else col == 1
-            goal = n_col - 1 if way == 0 else 0
 
             @pl.when(turn)
             def _():
+                if t == 0:
+                    target_copy(way).wait_recv()
                 for p in range(tiles):
                     for k in range(KD):
-                        pack[t][way, p * KD + k] = lbuf[t][left_index(goal, p, k, False)]
+                        pack[t][way, p * KD + k] = lbuf[t][left_index(tgt_end.at[way], p, k, False)]
                 slot_copy(way, t).start()
 
     def await_slots(t):
@@ -180,7 +182,7 @@
         for p in range(tiles):
             tests = sketch[p, :, t * piece : (t + 1) * piece]
             for k in range(KD):
-                coef = lbuf[t][left_index(col, p, k, True), 1]
+                coef = lbuf[t][left_index(tgt, p, k, True), 1]
                 pair = ubuf[t].at[up_index(p, k)]
                 middle = mul_t(coef, pair[0])
                 tested = mul_t(tests, pair[1])
@@ -191,9 +193,21 @@
                     acc_m[p, k] += middle
                     acc_v[p, k] += tested
 
+    tables = [
+        pltpu.make_async_copy(src, dst, tab_sem.at[i])
+        for i, (src, dst) in enumerate(((tgt_in, tgt), (lhome_in, lhome), (uhome_in, uhome), (sketch_in.at[0, 0], sketch)))
+    ]
+
+    def target_copy(way):
+        return pltpu.make_async_remote_copy(
+            src_ref=tgt_in, dst_ref=tgt_end.at[way], send_sem=ts_sem.at[way], recv_sem=tr_sem.at[way],
+            device_id=left_of if way == 0 else right, device_id_type=mesh_id)
+
     for t in range(pieces):
         for copy in local(t):
             copy.start()
+    for copy in tables:
+        copy.start()
 
     barrier = pltpu.get_barrier_semaphore()
     peers = [twin] + ([after, before] if n_row > 1 else [])
@@ -208,8 +222,15 @@
             greeted = greeted + able.astype(jnp.int32)
     pl.semaphore_wait(barrier, greeted)
 
+    if n_col > 2:
+        for way in range(2):
+            @pl.when(col == n_col - 1 if way == 0 else col == 0)
+            def _():
+                target_copy(way).start()
     for t in range(min(AHEAD, pieces)):
         send_own(t)
+    for copy in tables:
+        copy.wait()
     lag = max(n_col - 2, half_way - 1, 0)
     for step in range(pieces + lag):
         for dist in range(1, max(far, half_way) + 1):
@@ -240,7 +261,7 @@
             accumulate(step - lag)
 
     def row_basis(t, p):
-        return jnp.concatenate([lbuf[t][left_index(col, p, k, True), 0] for k in range(KD)], axis=0)
+        return jnp.concatenate([lbuf[t][left_index(tgt, p, k, True), 0] for k in range(KD)], axis=0)
 
     def twin_copy(which, src, dst):
         return pltpu.make_async_remote_copy(
@@ -292,6 +313,11 @@
     for i in range(owned):
         out_w[i] = (out_w[i] + hrecv[i]) / root
 
+    if n_col > 2:
+        for way in range(2):
+            @pl.when(col == n_col - 1 if way == 0 else col == 0)
+            def _():
+                target_copy(way).wait_send()
     for t in range(pieces):
         for way in range(2):
             for dist in range(1, far + 1):
@@ -318,17 +344,16 @@
         slots = tiles * KD
         owned = tiles // n_depth
         piece = width // PIECES
-        all_targets = lax.all_gather(targets[0], "col", axis=0, tiled=True)
         f32 = jnp.float32
         dma = pltpu.SemaphoreType.DMA
         far, half_way = max(n_col - 2, 1), max(n_row // 2, 1)
         out = jax.ShapeDtypeStruct((owned, rank, width), f32)
-        vmem, smem = pl.BlockSpec(memory_space=pltpu.VMEM), pl.BlockSpec(memory_space=pltpu.SMEM)
+        vmem, smem = pl.BlockSpec(memory_space=pltpu.VMEM), pltpu.SMEM
         anywhere = pl.BlockSpec(memory_space=pl.ANY)
         basis, weights = pl.pallas_call(
             functools.partial(kernel, sizes),
             out_shape=(out, out),
-            in_specs=[smem, smem, smem, anywhere, anywhere, vmem],
+            in_specs=[anywhere] * 6,
             out_specs=(vmem, vmem),
             scratch_shapes=[pltpu.VMEM((n_col * lheld + slots, 2, rank, piece), f32)] * PIECES
             + [pltpu.VMEM((n_row * uheld, 2, rank, piece), f32)] * PIECES
@@ -342,6 +367,14 @@
                 pltpu.VMEM((owned, rank, width), f32),
                 pltpu.VMEM((tiles, rank, KD * rank), f32),
                 pltpu.VMEM((tiles, rank, rank), f32),
+                smem(targets.shape, jnp.int32),
+                smem((2,) + targets.shape, jnp.int32),
+                smem(left_home.shape, jnp.int32),
+                smem(up_home.shape, jnp.int32),
+                pltpu.VMEM(sketch.shape[2:], f32),
+                dma((4,)),
+                dma((2,)),
+                dma((2,)),
                 dma((2, PIECES)),
                 dma((2, far, PIECES)),
                 dma((2, far, PIECES)),
@@ -353,8 +386,8 @@
                 dma((tiles + 1,)),
             ],
             compiler_params=pltpu.CompilerParams(
-                collective_id=0, has_side_effects=True, vmem_limit_bytes=48 * 1024 * 1024),
-        )(all_targets, left_home[0, 0], up_home[0, 0], left_store[0, 0], up_store[0, 0], sketch[0, 0])
+                collective_id=0, has_side_effects=True, vmem_limit_bytes=60 * 1024 * 1024),
+        )(targets, left_home, up_home, left_store, up_store, sketch)
         return basis[None, None], weights[None, None]
 
     return jax.shard_map(

time: 137 us -> 126 us (0.920)
  blocking collectives: 12.7 us -> 0 us
  Pallas kernels: 116 us -> 122 us
  local copies, waits for them, and re-layouts: 6.94 us -> 3.34 us
    all_gather x1 -> x0, blocking collectives: 12.7 us -> none  [shards(): all_targets = lax.all_gather(targets[0], 'col', axis=0, tiled=True)]
    pallas_call x1, Pallas kernels: 116 us -> 122 us  [shards(): pl.pallas_call(functools.partial(kernel, sizes), out_shape=(out, out), in...]
    unnamed x12 -> x2, local copies, waits for them, and re-layouts: 6.94 us -> 3.34 us
where the time goes in v2:
time: 126 us
  Pallas kernels  122 us (97%)
  local copies, waits for them, and re-layouts  3.34 us (3%)
    pallas_call x1, Pallas kernels, shards(): pl.pallas_call(functools.partial(kernel, sizes), out_shape=(out, out), in...  122 us
    unnamed x2, local copies, waits for them, and re-layouts  3.34 us

profile of v2, /device:TPU:0, one launch (start us, length us, event | category | flops | bytes accessed | tf_op | source)
XLA Modules:
  0.0 125.7 jit_solution(6634427621666473025)
XLA Ops:
  0.6 121.7 %shard_map.77 = (f32[1,64,1024]{2,1,0:T(8,128)}, f32[1,64,1024]{2,1,0:T(8,128)}) custom-call(s32[1,1,2]{2,1,0:T(1,128)} %tgt_in.1, s32[1,1,16]{2,1,0:T(1,128)} %lhome_in.1, s32[1,1,16]{2,1,0:T(1,128)} %uhome_in.1, f32[1,1,4,2,64,1024]{5,4,3,2,1,0:T(8,128)} %left_in.1, f32[1,1,4,2,64,1024]{5,4,3,2,1,0:T(8,128)} %up_in.1, f32[1,1,2,64,1024]{4,3,2,1,0:T(8,128)} %sketch_in.1), custom_call_target="tpu_custom_call" | custom-call | tf_op jit(solution)/shard_map/pallas_call | solution.py:353
  122.3 1.7 %copy.10 = f32[1,1,1,64,1024]{4,3,2,1,0:T(8,128)} copy(f32[1,1,1,64,1024]{4,3,2,1,0:T(8,128)} %bitcast.3) | data formatting | bytes 524288
  124.0 1.7 %copy.11 = f32[1,1,1,64,1024]{4,3,2,1,0:T(8,128)} copy(f32[1,1,1,64,1024]{4,3,2,1,0:T(8,128)} %bitcast.2) | data formatting | bytes 524288

commit v3 on v2

--- a/solution.py
+++ b/solution.py
@@ -11,8 +11,8 @@
 KD = 2
 RB = 8
 CB = 8
-PIECES = 4
-AHEAD = 2
+PIECES = 8
+AHEAD = 3
 HIGH = lax.Precision.HIGHEST
 
 

time: 126 us -> 124 us (0.984)
  Pallas kernels: 122 us -> 119 us
    pallas_call x1, Pallas kernels: 122 us -> 119 us  [shards(): pl.pallas_call(functools.partial(kernel, sizes), out_shape=(out, out), in...]
where the time goes in v3:
time: 124 us; the launch traced here: 123 us
  Pallas kernels  119 us (96%)
  local copies, waits for them, and re-layouts  3.34 us (3%)
    pallas_call x1, Pallas kernels, shards(): pl.pallas_call(functools.partial(kernel, sizes), out_shape=(out, out), in...  119 us
    unnamed x2, local copies, waits for them, and re-layouts  3.34 us

profile of v3, /device:TPU:0, one launch (start us, length us, event | category | flops | bytes accessed | tf_op | source)
XLA Modules:
  0.0 123.4 jit_solution(5074148389869196177)
XLA Ops:
  0.6 119.4 %shard_map.77 = (f32[1,64,1024]{2,1,0:T(8,128)}, f32[1,64,1024]{2,1,0:T(8,128)}) custom-call(s32[1,1,2]{2,1,0:T(1,128)} %tgt_in.1, s32[1,1,16]{2,1,0:T(1,128)} %lhome_in.1, s32[1,1,16]{2,1,0:T(1,128)} %uhome_in.1, f32[1,1,4,2,64,1024]{5,4,3,2,1,0:T(8,128)} %left_in.1, f32[1,1,4,2,64,1024]{5,4,3,2,1,0:T(8,128)} %up_in.1, f32[1,1,2,64,1024]{4,3,2,1,0:T(8,128)} %sketch_in.1), custom_call_target="tpu_custom_call" | custom-call | tf_op jit(solution)/shard_map/pallas_call | solution.py:353
  120.1 1.7 %copy.10 = f32[1,1,1,64,1024]{4,3,2,1,0:T(8,128)} copy(f32[1,1,1,64,1024]{4,3,2,1,0:T(8,128)} %bitcast.3) | data formatting | bytes 524288
  121.7 1.7 %copy.11 = f32[1,1,1,64,1024]{4,3,2,1,0:T(8,128)} copy(f32[1,1,1,64,1024]{4,3,2,1,0:T(8,128)} %bitcast.2) | data formatting | bytes 524288

commit v4 on v3

--- a/solution.py
+++ b/solution.py
@@ -12,7 +12,7 @@
 RB = 8
 CB = 8
 PIECES = 8
-AHEAD = 3
+AHEAD = 4
 HIGH = lax.Precision.HIGHEST
 
 
@@ -66,10 +66,11 @@
 def kernel(sizes, tgt_in, lhome_in, uhome_in, left_in, up_in, sketch_in, out_b, out_w, *scratch):
     n_row, n_col, n_depth = sizes
     pieces = PIECES
-    lbuf, scratch = scratch[:pieces], scratch[pieces:]
+    units = 2 * pieces
+    lbuf, scratch = scratch[:units], scratch[units:]
+    pack, scratch = scratch[:units], scratch[units:]
     ubuf, scratch = scratch[:pieces], scratch[pieces:]
-    pack, scratch = scratch[:pieces], scratch[pieces:]
-    (acc_m, acc_v, zpart, zrecv, hpart, hrecv, inner, linv,
+    (acc_m, acc_v, acc_g, acc_s, zpart, zrecv, hpart, hrecv, inner, linv,
      tgt, tgt_end, lhome, uhome, sketch, tab_sem, ts_sem, tr_sem, loc_sem, zs_sem, zr_sem, rs_sem, rr_sem, ks_sem, kr_sem, xs_sem, xr_sem) = scratch
     left, up = left_in.at[0, 0], up_in.at[0, 0]
     lheld, uheld = left.shape[0], up.shape[0]
@@ -90,12 +91,14 @@
     twin = (row, col, other)
     mesh_id = pl.DeviceIdType.MESH
 
-    def local(t):
+    def local_line(u):
+        factor = 1 if u < pieces else 0
+        cut = pl.ds((u % pieces) * piece, piece)
+        return pltpu.make_async_copy(left.at[:, factor, :, cut], lbuf[u].at[pl.ds(col * lheld, lheld)], loc_sem.at[u])
+
+    def local_ring(t):
         cut = pl.ds(t * piece, piece)
-        return (
-            pltpu.make_async_copy(left.at[:, :, :, cut], lbuf[t].at[pl.ds(col * lheld, lheld)], loc_sem.at[0, t]),
-            pltpu.make_async_copy(up.at[:, :, :, cut], ubuf[t].at[pl.ds(row * uheld, uheld)], loc_sem.at[1, t]),
-        )
+        return pltpu.make_async_copy(up.at[:, :, :, cut], ubuf[t].at[pl.ds(row * uheld, uheld)], loc_sem.at[units + t])
 
     def line_copy(way, dist, t):
         source = col - (dist - 1) if way == 0 else col + (dist - 1)
@@ -148,14 +151,17 @@
     def up_index(p, k):
         return uhome[0, 0, (tgt[0, 0, p] % CB) * KD + k]
 
-    def send_own(t):
-        for copy in local(t):
-            copy.wait()
+    def send_line(u):
+        local_line(u).wait()
         for way in range(2):
             if n_col > 1:
                 @pl.when(can_send(way, 1))
                 def _():
-                    line_copy(way, 1, t).start()
+                    line_copy(way, 1, u).start()
+
+    def send_ring(t):
+        local_ring(t).wait()
+        for way in range(2):
             if n_row > 1:
                 ring_copy(way, 1, t).start()
 
@@ -182,7 +188,7 @@
         for p in range(tiles):
             tests = sketch[p, :, t * piece : (t + 1) * piece]
             for k in range(KD):
-                coef = lbuf[t][left_index(tgt, p, k, True), 1]
+                coef = lbuf[t][left_index(tgt, p, k, True)]
                 pair = ubuf[t].at[up_index(p, k)]
                 middle = mul_t(coef, pair[0])
                 tested = mul_t(tests, pair[1])
@@ -203,9 +209,10 @@
             src_ref=tgt_in, dst_ref=tgt_end.at[way], send_sem=ts_sem.at[way], recv_sem=tr_sem.at[way],
             device_id=left_of if way == 0 else right, device_id_type=mesh_id)
 
-    for t in range(pieces):
-        for copy in local(t):
-            copy.start()
+    for u in range(units):
+        local_line(u).start()
+        if u < pieces:
+            local_ring(u).start()
     for copy in tables:
         copy.start()
 
@@ -227,63 +234,90 @@
             @pl.when(col == n_col - 1 if way == 0 else col == 0)
             def _():
                 target_copy(way).start()
-    for t in range(min(AHEAD, pieces)):
-        send_own(t)
+    def row_basis(t, p):
+        return jnp.concatenate([lbuf[pieces + t][left_index(tgt, p, k, True)] for k in range(KD)], axis=0)
+
+    def twin_copy(which, src, dst):
+        return pltpu.make_async_remote_copy(
+            src_ref=src, dst_ref=dst, send_sem=xs_sem.at[which], recv_sem=xr_sem.at[which], device_id=twin, device_id_type=mesh_id)
+
+    def z_copy(t):
+        return twin_copy(t, zpart.at[t], zrecv.at[t])
+
+    def fold():
+        for p in range(tiles):
+            inner[p] = jnp.concatenate([mul_t(acc_v[p, k], acc_m[p, k]) for k in range(KD)], axis=1)
+
+    def sample(t):
+        for p in range(tiles):
+            zpart[t, p] = mul(inner[p], row_basis(t, p))
+        z_copy(t).start()
+
+    def gather_grams(t):
+        z_copy(t).wait()
+        for p in range(tiles):
+            z = zpart[t, p] + zrecv[t, p]
+            zpart[t, p] = z
+            g, s = mul_t(z, z), mul_t(z, row_basis(t, p))
+            if t == 0:
+                acc_g[p] = g
+                acc_s[p] = s
+            else:
+                acc_g[p] += g
+                acc_s[p] += s
+
+    ring_at = [(3 * t) // 2 for t in range(pieces)]
+    for u in range(min(AHEAD, units)):
+        send_line(u)
+        for t in range(pieces):
+            if ring_at[t] == u:
+                send_ring(t)
     for copy in tables:
         copy.wait()
-    lag = max(n_col - 2, half_way - 1, 0)
-    for step in range(pieces + lag):
+    line_lag, ring_lag = max(n_col - 2, 0), max(half_way - 1, 0)
+    lag = max(line_lag, ring_lag)
+    sampled = 0
+    for step in range(units + lag):
         for dist in range(1, max(far, half_way) + 1):
-            t = step - (dist - 1)
-            if not 0 <= t < pieces:
-                continue
+            u = step - (dist - 1)
             for way in range(2):
-                if dist <= far:
+                if dist <= far and 0 <= u < units:
                     @pl.when(receives(way, dist))
                     def _():
-                        line_copy(way, dist, t).wait_recv()
+                        line_copy(way, dist, u).wait_recv()
                     if dist + 1 <= far:
                         @pl.when(can_send(way, dist + 1))
                         def _():
-                            line_copy(way, dist + 1, t).start()
-                if n_row > 1 and dist <= half_way:
+                            line_copy(way, dist + 1, u).start()
+                if n_row > 1 and dist <= half_way and u in ring_at:
+                    t = ring_at.index(u)
                     ring_copy(way, dist, t).wait_recv()
                     if dist + 1 <= half_way:
                         ring_copy(way, dist + 1, t).start()
-        if AHEAD + step < pieces:
-            send_own(AHEAD + step)
+        if AHEAD + step < units:
+            send_line(AHEAD + step)
+            if AHEAD + step in ring_at:
+                send_ring(ring_at.index(AHEAD + step))
         if n_col > 2:
-            if 0 <= step - (n_col - 3) < pieces:
+            if 0 <= step - (n_col - 3) < units:
                 fill_slots(step - (n_col - 3))
-            if 0 <= step - (n_col - 2) < pieces:
+            if 0 <= step - (n_col - 2) < units:
                 await_slots(step - (n_col - 2))
-        if 0 <= step - lag < pieces:
-            accumulate(step - lag)
-
-    def row_basis(t, p):
-        return jnp.concatenate([lbuf[t][left_index(tgt, p, k, True), 0] for k in range(KD)], axis=0)
-
-    def twin_copy(which, src, dst):
-        return pltpu.make_async_remote_copy(
-            src_ref=src, dst_ref=dst, send_sem=xs_sem.at[which], recv_sem=xr_sem.at[which], device_id=twin, device_id_type=mesh_id)
-
-    z_copies = [twin_copy(p, zpart.at[p], zrecv.at[p]) for p in range(tiles)]
-    for p in range(tiles):
-        folded = jnp.concatenate([mul_t(acc_v[p, k], acc_m[p, k]) for k in range(KD)], axis=1)
-        for t in range(pieces):
-            zpart[p, :, t * piece : (t + 1) * piece] = mul(folded, row_basis(t, p))
-        z_copies[p].start()
-    grams, sides = [], []
-    for p in range(tiles):
-        z_copies[p].wait()
-        zpart[p] = zpart[p] + zrecv[p]
-        gram, side = None, None
-        for t in range(pieces):
-            z = zpart[p, :, t * piece : (t + 1) * piece]
-            g, s = mul_t(z, z), mul_t(z, row_basis(t, p))
-            gram, side = (g, s) if t == 0 else (gram + g, side + s)
-        grams.append(gram)
-        sides.append(side)
+        u = step - lag
+        if u in ring_at:
+            accumulate(ring_at.index(u))
+        if u == ring_at[-1]:
+            fold()
+        elif u > ring_at[-1]:
+            ready = u - pieces + 1
+            for t in range(sampled, ready):
+                sample(t)
+                if t > 0:
+                    gather_grams(t - 1)
+            sampled = ready
+    gather_grams(pieces - 1)
+    grams = [acc_g[p] for p in range(tiles)]
+    sides = [acc_s[p] for p in range(tiles)]
     inverses = inverse_factor(grams)
     for p in range(tiles):
         linv[p] = inverses[p]
@@ -298,7 +332,7 @@
         cols = jnp.concatenate([ubuf[t][up_index(p, k), 1] for k in range(KD)], axis=0)
         return mul(inner[p], cols)
 
-    h_copy = twin_copy(tiles, hpart, hrecv)
+    h_copy = twin_copy(pieces, hpart, hrecv)
     for i in range(owned):
         for t in range(pieces):
             hpart[i, :, t * piece : (t + 1) * piece] = project(other * owned + i, t)
@@ -307,7 +341,7 @@
         p = dep * owned + i
         for t in range(pieces):
             cut = slice(t * piece, (t + 1) * piece)
-            out_b[i, :, cut] = mul(linv[p], zpart[p, :, cut]) * root
+            out_b[i, :, cut] = mul(linv[p], zpart[t, p]) * root
             out_w[i, :, cut] = project(p, t)
     h_copy.wait()
     for i in range(owned):
@@ -318,7 +352,7 @@
             @pl.when(col == n_col - 1 if way == 0 else col == 0)
             def _():
                 target_copy(way).wait_send()
-    for t in range(pieces):
+    for t in range(units):
         for way in range(2):
             for dist in range(1, far + 1):
                 @pl.when(can_send(way, dist))
@@ -328,7 +362,7 @@
                 @pl.when(col == n_col - 2 if way == 0 else col == 1)
                 def _():
                     slot_copy(way, t).wait_send()
-            if n_row > 1:
+            if n_row > 1 and t < pieces:
                 for dist in range(1, half_way + 1):
                     ring_copy(way, dist, t).wait_send()
 
@@ -343,7 +377,7 @@
         tiles = targets.shape[2]
         slots = tiles * KD
         owned = tiles // n_depth
-        piece = width // PIECES
+        piece, units = width // PIECES, 2 * PIECES
         f32 = jnp.float32
         dma = pltpu.SemaphoreType.DMA
         far, half_way = max(n_col - 2, 1), max(n_row // 2, 1)
@@ -355,14 +389,16 @@
             out_shape=(out, out),
             in_specs=[anywhere] * 6,
             out_specs=(vmem, vmem),
-            scratch_shapes=[pltpu.VMEM((n_col * lheld + slots, 2, rank, piece), f32)] * PIECES
+            scratch_shapes=[pltpu.VMEM((n_col * lheld + slots, rank, piece), f32)] * units
+            + [pltpu.VMEM((2, slots, rank, piece), f32)] * units
             + [pltpu.VMEM((n_row * uheld, 2, rank, piece), f32)] * PIECES
-            + [pltpu.VMEM((2, slots, 2, rank, piece), f32)] * PIECES
             + [
                 pltpu.VMEM((tiles, KD, rank, rank), f32),
                 pltpu.VMEM((tiles, KD, rank, rank), f32),
-                pltpu.VMEM((tiles, rank, width), f32),
-                pltpu.VMEM((tiles, rank, width), f32),
+                pltpu.VMEM((tiles, rank, rank), f32),
+                pltpu.VMEM((tiles, rank, KD * rank), f32),
+                pltpu.VMEM((PIECES, tiles, rank, piece), f32),
+                pltpu.VMEM((PIECES, tiles, rank, piece), f32),
                 pltpu.VMEM((owned, rank, width), f32),
                 pltpu.VMEM((owned, rank, width), f32),
                 pltpu.VMEM((tiles, rank, KD * rank), f32),
@@ -375,15 +411,15 @@
                 dma((4,)),
                 dma((2,)),
                 dma((2,)),
-                dma((2, PIECES)),
-                dma((2, far, PIECES)),
-                dma((2, far, PIECES)),
+                dma((units + PIECES,)),
+                dma((2, far, units)),
+                dma((2, far, units)),
                 dma((2, half_way, PIECES)),
                 dma((2, half_way, PIECES)),
-                dma((2, PIECES)),
-                dma((2, PIECES)),
-                dma((tiles + 1,)),
-                dma((tiles + 1,)),
+                dma((2, units)),
+                dma((2, units)),
+                dma((PIECES + 1,)),
+                dma((PIECES + 1,)),
             ],
             compiler_params=pltpu.CompilerParams(
                 collective_id=0, has_side_effects=True, vmem_limit_bytes=60 * 1024 * 1024),

time: 124 us -> 126 us (1.016)
  Pallas kernels: 119 us -> 122 us
    pallas_call x1, Pallas kernels: 119 us -> 122 us  [shards(): pl.pallas_call(functools.partial(kernel, sizes), out_shape=(out, out), in...]
where the time goes in v4:
time: 126 us
  Pallas kernels  122 us (97%)
  local copies, waits for them, and re-layouts  3.34 us (3%)
    pallas_call x1, Pallas kernels, shards(): pl.pallas_call(functools.partial(kernel, sizes), out_shape=(out, out), in...  122 us
    unnamed x2, local copies, waits for them, and re-layouts  3.34 us

profile of v4, /device:TPU:0, one launch (start us, length us, event | category | flops | bytes accessed | tf_op | source)
XLA Modules:
  0.0 125.7 jit_solution(8968997204028147506)
XLA Ops:
  0.6 121.7 %shard_map.77 = (f32[1,64,1024]{2,1,0:T(8,128)}, f32[1,64,1024]{2,1,0:T(8,128)}) custom-call(s32[1,1,2]{2,1,0:T(1,128)} %tgt_in.1, s32[1,1,16]{2,1,0:T(1,128)} %lhome_in.1, s32[1,1,16]{2,1,0:T(1,128)} %uhome_in.1, f32[1,1,4,2,64,1024]{5,4,3,2,1,0:T(8,128)} %left_in.1, f32[1,1,4,2,64,1024]{5,4,3,2,1,0:T(8,128)} %up_in.1, f32[1,1,2,64,1024]{4,3,2,1,0:T(8,128)} %sketch_in.1), custom_call_target="tpu_custom_call" | custom-call | tf_op jit(solution)/shard_map/pallas_call | solution.py:387
  122.4 1.7 %copy.10 = f32[1,1,1,64,1024]{4,3,2,1,0:T(8,128)} copy(f32[1,1,1,64,1024]{4,3,2,1,0:T(8,128)} %bitcast.3) | data formatting | bytes 524288
  124.0 1.7 %copy.11 = f32[1,1,1,64,1024]{4,3,2,1,0:T(8,128)} copy(f32[1,1,1,64,1024]{4,3,2,1,0:T(8,128)} %bitcast.2) | data formatting | bytes 524288

commit v5 on v4

--- a/solution.py
+++ b/solution.py
@@ -12,7 +12,7 @@
 RB = 8
 CB = 8
 PIECES = 8
-AHEAD = 4
+AHEAD = 2
 HIGH = lax.Precision.HIGHEST
 
 

time: 126 us -> 120 us (0.952)
  Pallas kernels: 122 us -> 116 us
    pallas_call x1, Pallas kernels: 122 us -> 116 us  [shards(): pl.pallas_call(functools.partial(kernel, sizes), out_shape=(out, out), in...]
where the time goes in v5:
time: 120 us
  Pallas kernels  116 us (97%)
  local copies, waits for them, and re-layouts  3.34 us (3%)
    pallas_call x1, Pallas kernels, shards(): pl.pallas_call(functools.partial(kernel, sizes), out_shape=(out, out), in...  116 us
    unnamed x2, local copies, waits for them, and re-layouts  3.34 us

profile of v5, /device:TPU:0, one launch (start us, length us, event | category | flops | bytes accessed | tf_op | source)
XLA Modules:
  0.0 120.2 jit_solution(6744148983535687360)
XLA Ops:
  0.6 116.3 %shard_map.77 = (f32[1,64,1024]{2,1,0:T(8,128)}, f32[1,64,1024]{2,1,0:T(8,128)}) custom-call(s32[1,1,2]{2,1,0:T(1,128)} %tgt_in.1, s32[1,1,16]{2,1,0:T(1,128)} %lhome_in.1, s32[1,1,16]{2,1,0:T(1,128)} %uhome_in.1, f32[1,1,4,2,64,1024]{5,4,3,2,1,0:T(8,128)} %left_in.1, f32[1,1,4,2,64,1024]{5,4,3,2,1,0:T(8,128)} %up_in.1, f32[1,1,2,64,1024]{4,3,2,1,0:T(8,128)} %sketch_in.1), custom_call_target="tpu_custom_call" | custom-call | tf_op jit(solution)/shard_map/pallas_call | solution.py:387
  116.9 1.7 %copy.10 = f32[1,1,1,64,1024]{4,3,2,1,0:T(8,128)} copy(f32[1,1,1,64,1024]{4,3,2,1,0:T(8,128)} %bitcast.3) | data formatting | bytes 524288
  118.6 1.7 %copy.11 = f32[1,1,1,64,1024]{4,3,2,1,0:T(8,128)} copy(f32[1,1,1,64,1024]{4,3,2,1,0:T(8,128)} %bitcast.2) | data formatting | bytes 524288
